TPU v7x, 32 devices: a whole 2x2x4 slice. The times are simulated.
32 devices in a mesh: fsdp: 2 (over x), ctx: 4 (over z), tp: 4 (over y, core).
Axes of the slice: x: 2, y: 2, z: 4, core: 2. Of those that a mesh axis runs over, the one named last changes fastest.
Arguments:
- inputs: bfloat16 [4, 736, 1152], P('fsdp', 'ctx'), may hold values from -6 to 6
- cotangent: bfloat16 [4, 736, 1152], P('fsdp', 'ctx'), may hold values from -6 to 6
- valid_count: int32 [4], P('fsdp'), may hold values from 369 to 736, as said below
- norm_gain: float32 [2, 2, 1152], replicated, may hold values from 0.5 to 1.5
- norm_bias: float32 [2, 2, 1152], replicated, may hold values from -1.8 to 1.8
- w_qkv: bfloat16 [2, 1152, 3, 1152], P(None, ('fsdp', 'ctx'), None, 'tp'), may hold values from -0.25 to 0.25
- bias_qv: float32 [2, 2, 1152], P(None, None, 'tp'), may hold values from -3 to 3
- w_out: bfloat16 [2, 1152, 1152], P(None, ('fsdp', 'ctx'), 'tp'), may hold values from -1.5 to 1.5
- w_up: bfloat16 [2, 1152, 4304], P(None, ('fsdp', 'ctx'), 'tp'), may hold values from -0.1875 to 0.1875
- bias_up: float32 [2, 4304], P(None, 'tp'), may hold values from -3 to 3
- w_down: bfloat16 [2, 1152, 4304], P(None, ('fsdp', 'ctx'), 'tp'), may hold values from -0.09375 to 0.09375
- bias_resid: float32 [2, 2, 1152], replicated, may hold values from -1.8 to 1.8
Outputs:
- output: bfloat16 [4, 736, 1152], P('fsdp', 'ctx')
- grad_inputs: float32 [4, 736, 1152], P('fsdp', 'ctx')
- grad_norm_gain: float32 [2, 2, 1152], replicated
- grad_norm_bias: float32 [2, 2, 1152], replicated
- grad_qkv: float32 [2, 1152, 3, 1152], P(None, ('fsdp', 'ctx'), None, 'tp')
- grad_bias_qv: float32 [2, 2, 1152], P(None, None, 'tp')
- grad_out: float32 [2, 1152, 1152], P(None, ('fsdp', 'ctx'), 'tp')
- grad_up: float32 [2, 1152, 4304], P(None, ('fsdp', 'ctx'), 'tp')
- grad_bias_up: float32 [2, 4304], P(None, 'tp')
- grad_down: float32 [2, 1152, 4304], P(None, ('fsdp', 'ctx'), 'tp')
- grad_bias_resid: float32 [2, 2, 1152], replicated
Inputs may be any that keep to these rules, and one draw needn't show every extreme that they name: `valid_count`: some image has no padding.
All inputs are finite; a program needn't handle non-finite values.
Results may differ from a plain program's by a relative error of at most 0.028.
The roundings to bfloat16 on the way count: a program that leaves them out, or rounds other values in their place, can miss the bound.
Values may be sent and summed in bfloat16 or wider, within the bound.
A program may use at most 192 MiB of HBM per device.

v0:
```python
import functools

import jax
import jax.numpy as jnp
from jax import lax
from jax.experimental import pallas as pl
from jax.experimental.pallas import tpu as pltpu
from jax.sharding import PartitionSpec as P

HEAD_DIM = 72
norm_eps = 1e-06
gelu_root = 0.7978845608028654
gelu_cubic = 0.044715
masked_score = -1e30
LOG2_E = 1.4426950408889634

MESH = pl.DeviceIdType.MESH
f32 = jnp.float32
bf16 = jnp.bfloat16
VMEM = pltpu.VMEM
DMA = pltpu.SemaphoreType.DMA


def up_to(value, unit):
    return (value + unit - 1) // unit * unit


def dot(a, b, over):
    return lax.dot_general(a, b, (((over[0],), (over[1],)), ((), ())), preferred_element_type=f32)


class Sizes:
    def __init__(self, mesh, inputs, w_qkv, w_up):
        self.fsdp, self.ctx, self.tp = mesh.shape["fsdp"], mesh.shape["ctx"], mesh.shape["tp"]
        self.images, self.rows, self.d = inputs.shape
        self.layers, self.wrows = w_qkv.shape[0], w_qkv.shape[1]
        self.zl = self.ctx // self.images
        self.chips_y = self.tp // 2
        self.chips = self.zl * self.chips_y
        self.team = self.chips * 2
        self.part = up_to(-(-self.rows // self.tp), 16)
        self.block = self.images * self.part
        self.units = self.chips * self.images
        self.half = self.units * self.part
        self.tile = 2 * self.part
        self.steps = self.units // 2
        self.keys = 2 * self.half
        self.wide = w_qkv.shape[3] // self.zl
        self.heads = self.wide // HEAD_DIM
        self.ff = w_up.shape[2] // self.zl
        self.headp = up_to(self.wide, 128)
        self.qkvp = up_to(3 * self.wide, 128)
        self.attnp = up_to(4 * self.wide, 128)
        self.spare = self.attnp - 4 * self.wide
        self.ff_at = 4 * self.wide % 128
        self.ff_sent = 128 if self.spare else 0
        end = self.ff_at + self.ff
        self.ffw = up_to(end + self.ff, 128)
        self.ffs = self.ffw - self.ff_sent
        self.down_at = end // 128 * 128
        self.down_shift = end - self.down_at
        self.ffp = self.ffw - self.down_at
        assert up_to(end, 128) <= self.ffp and self.spare < self.ff
        self.wrowsp = up_to(self.wrows, 16)
        self.chunk = 48 if self.wrowsp % 48 == 0 else self.wrowsp
        self.chunks = self.wrowsp // self.chunk
        self.groups = self.fsdp * self.ctx


class Place:
    def __init__(self, sz):
        self.sz = sz
        self.f, self.c, self.t = lax.axis_index("fsdp"), lax.axis_index("ctx"), lax.axis_index("tp")
        self.zh, self.zl = self.c // sz.zl, self.c % sz.zl
        self.y, self.k = self.t // 2, self.t % 2
        self.chip = self.zl * sz.chips_y + self.y
        self.slot = 2 * self.chip + self.k

    def chip_at(self, step):
        sz = self.sz
        zl = (self.zl + step // sz.chips_y) % sz.zl
        y = (self.y + step % sz.chips_y) % sz.chips_y
        return zl, y

    def chip_back(self, step):
        sz = self.sz
        zl = (self.zl + sz.zl - step // sz.chips_y) % sz.zl
        y = (self.y + sz.chips_y - step % sz.chips_y) % sz.chips_y
        return zl, y

    def index(self, chip):
        return chip[0] * self.sz.chips_y + chip[1]

    def device(self, chip):
        return (self.f, self.zh * self.sz.zl + chip[0], 2 * chip[1] + self.k)

    @property
    def twin(self):
        return (self.f, self.c, self.t + 1 - 2 * self.k)


    def ctx_ahead(self, step):
        sz = self.sz
        return (self.zh + step // sz.zl) % sz.images * sz.zl + (self.zl + step % sz.zl) % sz.zl

    def ctx_back(self, step):
        sz = self.sz
        zh = (self.zh + sz.images - step // sz.zl) % sz.images
        return zh * sz.zl + (self.zl + sz.zl - step % sz.zl) % sz.zl


def split_refs(refs, *counts):
    out, at = [], 0
    for count in counts:
        out.append(refs[at:at + count])
        at += count
    assert at == len(refs)
    return out


class Greeting:
    def __init__(self, others):
        self.count = len(others)
        self.barrier = pltpu.get_barrier_semaphore()
        for other in others:
            pl.semaphore_signal(self.barrier, inc=1, device_id=other, device_id_type=MESH)

    def wait(self):
        pl.semaphore_wait(self.barrier, self.count)


def send(src, dst, send_sem, recv_sem, device):
    return pltpu.make_async_remote_copy(
        src_ref=src, dst_ref=dst, send_sem=send_sem, recv_sem=recv_sem, device_id=device, device_id_type=MESH
    )


def team_peers(pc):
    return [pc.device(pc.chip_at(step)) for step in range(1, pc.sz.chips)] + [pc.twin]


def line_peers(pc):
    sz = pc.sz
    return [(pc.f, pc.c, 2 * ((pc.y + dy) % sz.chips_y) + 1 - pc.k) for dy in range(1, sz.chips_y)]


def weight_peers(pc, team=False):
    sz = pc.sz
    first = sz.zl if team else 1
    return [(pc.f, pc.ctx_ahead(step), pc.t) for step in range(first, sz.ctx)] + [
        ((pc.f + jump) % sz.fsdp, pc.c, pc.t) for jump in range(1, sz.fsdp)
    ]


def pick(step, values):
    if isinstance(step, int):
        return values[step]
    out = jnp.int32(values[0])
    for i in range(1, len(values)):
        out = jnp.where(step == i, jnp.int32(values[i]), out)
    return out


def when(condition, run):
    if isinstance(condition, (bool, int)):
        if condition:
            run()
    else:
        pl.when(condition)(run)


FF_OVER = 3

FORWARD_TURN = (False, True)
BACKWARD_TURN = (True, False)
SUM_TURN = (True, True)


class Routes:
    def __init__(self, sz):
        self.sz = sz
        self.z = [dz * sz.chips_y for dz in range(1, sz.zl)]
        self.y = list(range(1, sz.chips_y))
        self.turned = [dz + dy for dz in self.z for dy in self.y]
        self.arriving = [0] + self.z + self.y + self.turned
        self.leaving = self.turned + self.y + self.z + [0]

    def at(self, order, step):
        per = len(order) // 2
        firsts, seconds = order[0::2] * self.sz.images, order[1::2] * self.sz.images
        pieces = [p for p in range(self.sz.images) for _ in range(per)]
        return pick(step, firsts), pick(step, seconds), pick(step, pieces)


class Gather:
    def __init__(self, pc, buf, sems, turn):
        self.pc, self.buf, self.sems, self.turn = pc, buf, sems, turn
        self.routes = Routes(pc.sz)

    def move(self, back, piece, at, device):
        return send(self.buf.at[at, piece], self.buf.at[at, piece], self.sems.at[0, back, piece],
                    self.sems.at[1, back, piece], device)

    def start(self, piece, low):
        pc, routes = self.pc, self.routes
        self.buf[pc.chip, piece] = low
        for step in routes.z + routes.y + ([] if self.turn else routes.turned):
            self.move(step, piece, pc.chip, pc.device(pc.chip_at(step))).start()

    def ready(self, step):
        pc, sz = self.pc, self.pc.sz
        *chips, piece = self.routes.at(self.routes.arriving, step)
        places = []
        for back in chips:
            at = pc.index(pc.chip_back(back))
            when(back > 0, self.move(back, piece, at, pc.twin).wait_recv)
            if self.turn:
                for dz in self.routes.z:

                    def pass_on(dz=dz, at=at):
                        for dy in self.routes.y:
                            self.move(dz + dy, piece, at, pc.device(pc.chip_at(dy))).start()

                    when(back == dz, pass_on)
            places.append(at)
        tokens = jnp.concatenate([self.buf[at, piece] for at in places], axis=0)
        return [piece * sz.chips + at for at in places], tokens

    def finish(self):
        for piece in range(self.pc.sz.images):
            for back in self.routes.arriving[1:]:
                self.move(back, piece, self.pc.chip, self.pc.twin).wait_send()


class Scatter:
    def __init__(self, pc, bufs, sems, own_last, turn):
        self.pc, self.sems, self.turn = pc, sems, turn
        self.keep, self.hold, self.sent, self.got = bufs
        self.routes = Routes(pc.sz)
        self.order = self.routes.leaving if own_last else self.routes.arriving

    def far(self, back, piece):
        pc, sz = self.pc, self.pc.sz
        to = back
        if self.turn:
            if isinstance(back, int):
                to = back % sz.chips_y or back
            else:
                dy = lax.rem(back, jnp.int32(sz.chips_y))
                to = jnp.where(dy > 0, dy, back)
        return send(self.sent.at[back, piece], self.got.at[back, piece], self.sems.at[0, back, piece],
                    self.sems.at[1, back, piece], pc.device(pc.chip_back(to)))

    def units(self, step):
        pc = self.pc
        *chips, piece = self.routes.at(self.order, step)
        return [piece * pc.sz.chips + pc.index(pc.chip_back(back)) for back in chips]

    def push(self, step, partial):
        sz, part = self.pc.sz, self.pc.sz.part
        *chips, piece = self.routes.at(self.order, step)
        for i, back in enumerate(chips):
            terms = partial[i * part:(i + 1) * part]

            def own(terms=terms):
                self.keep[piece] = terms

            def leave(terms=terms, back=back):
                self.sent[back, piece] = terms.astype(bf16)
                self.far(back, piece).start()

            def hold(terms=terms, dz=None):
                self.hold[dz // sz.chips_y - 1] = terms

            when(back == 0, own)
            held = back < 0
            if self.turn:
                for dz in self.routes.z:
                    when(back == dz, functools.partial(hold, dz=dz))
                    held = held | (back == dz)
            when((back > 0) & jnp.logical_not(held), leave)
        if self.turn:
            per = sz.chips // 2
            for p in range(1, sz.images):
                when(step == p * per, functools.partial(self.merge, p - 1))

    def merge(self, piece):
        sz = self.pc.sz
        for dz in self.routes.z:
            total = self.hold[dz // sz.chips_y - 1]
            for dy in self.routes.y:
                self.far(dz + dy, piece).wait_recv()
                total = total + self.got[dz + dy, piece].astype(f32)
            self.sent[dz, piece] = total.astype(bf16)
            self.far(dz, piece).start()

    def flush(self):
        if self.turn:
            self.merge(self.pc.sz.images - 1)

    def finish(self, piece):
        total = self.keep[piece]
        for back in self.routes.z + self.routes.y + ([] if self.turn else self.routes.turned):
            self.far(back, piece).wait_recv()
            total = total + self.got[back, piece].astype(f32)
        for back in self.routes.arriving[1:]:
            self.far(back, piece).wait_send()
        return total


class Swap:
    def __init__(self, pc, src, dst, send_sem, recv_sem):
        self.copy = send(src, dst, send_sem, recv_sem, pc.twin)

    def start(self):
        self.copy.start()

    def wait(self):
        self.copy.wait()


def team_scratch(sz, phases):
    n = (sz.chips, sz.images)
    return [
        VMEM((sz.images, sz.part, sz.d), f32),
        VMEM((max(sz.zl - 1, 1), sz.part, sz.d), f32),
        VMEM(n + (sz.part, sz.d), bf16),
        VMEM(n + (sz.part, sz.d), bf16),
        DMA((phases, 2) + n),
        DMA((phases, 2) + n),
    ]


def normalised(values):
    centre = jnp.mean(values, axis=-1, keepdims=True)
    centred = values - centre
    spread = jnp.mean(centred * centred, axis=-1, keepdims=True)
    inverse = lax.rsqrt(spread + norm_eps)
    return centred * inverse, inverse


def norm_back(values, gain, grad):
    high, inverse = normalised(values)
    scaled = grad * gain
    term = inverse * (
        scaled
        - jnp.mean(scaled, axis=-1, keepdims=True)
        - high * jnp.mean(scaled * high, axis=-1, keepdims=True)
    )
    return term, jnp.sum(grad * high, axis=0, keepdims=True), jnp.sum(grad, axis=0, keepdims=True)


def lanes_of(shape):
    return lax.broadcasted_iota(jnp.int32, shape, len(shape) - 1)


def unpack_out(sz, w_ref, o_ref):
    at = 3 * sz.wide // 128 * 128
    shift = 3 * sz.wide - at

    def step(i, carry):
        rows = pl.ds(pl.multiple_of(i * 128, 128), 128)
        piece = pltpu.roll(w_ref[rows, at:at + sz.headp].astype(f32), sz.headp - shift, 1)
        o_ref[rows, :] = jnp.where(lanes_of(piece.shape) < sz.wide, piece, 0.0).astype(bf16)
        return carry

    lax.fori_loop(0, sz.d // 128, step, 0)


def take(sz, values, kind):
    at = kind * sz.wide // 128 * 128
    shift = kind * sz.wide - at
    piece = values[:, at:at + sz.headp]
    if shift:
        piece = pltpu.roll(piece, sz.headp - shift, 1)
    return jnp.where(lanes_of(piece.shape) < sz.wide, piece, 0.0)


def head_of(values, head):
    lanes = lanes_of(values.shape)
    mine = (lanes >= head * HEAD_DIM) & (lanes < (head + 1) * HEAD_DIM)
    return jnp.where(mine, values, jnp.zeros_like(values))


def probabilities(q_head, keys, valid):
    scores = jnp.where(valid > 0.0, dot(q_head, keys, (1, 1)), masked_score)
    high = jnp.max(scores, axis=-1, keepdims=True)
    weights = jnp.exp2((scores - high) * (HEAD_DIM ** (-0.5) * LOG2_E))
    return weights * (1.0 / jnp.sum(weights, axis=-1, keepdims=True))


class Jobs:
    def __init__(self, **places):
        self.places = places

    def run(self, place):
        for job in self.places.get(place, ()):
            job()

    def at(self, place, step):
        for when_step, jobs in self.places.get(place, {}).items():

            def run(jobs=jobs):
                for job in jobs:
                    job()

            when(step == when_step, run)


class Copies:
    def __init__(self, sems):
        self.sems, self.made = sems, []

    def start(self, src, dst):
        ident = len(self.made)
        self.made.append((src, dst))
        pltpu.make_async_copy(src, dst, self.sems.at[ident]).start()
        return ident

    def wait(self, idents=None):
        for ident in range(len(self.made)) if idents is None else idents:
            src, dst = self.made[ident]
            pltpu.make_async_copy(src, dst, self.sems.at[ident]).wait()


class Fetch:
    def __init__(self, pc, own, everything, sems, twin_sems, first=0):
        self.lanes = pl.ds(first, own.shape[-1])
        self.pc, self.own, self.all, self.sems, self.twin_sems = pc, own, everything, sems, twin_sems

    def rows(self, group, chunk):
        sz = self.pc.sz
        at = group * sz.wrowsp + chunk * sz.chunk
        return self.all.at[self.pc.k, pl.ds(pl.multiple_of(at, 16), sz.chunk), self.lanes]

    def own_rows(self, half, chunk):
        return self.own.at[half, pl.ds(chunk * self.pc.sz.chunk, self.pc.sz.chunk)]

    def along_ctx(self, step, chunk):
        pc = self.pc
        c = pc.ctx_ahead(step)
        return send(self.own_rows(c % pc.sz.zl, chunk), self.rows(pc.f * pc.sz.ctx + pc.c, chunk),
                    self.sems.at[chunk, 0, 0, step], self.sems.at[chunk, 0, 1, step], (pc.f, c, pc.t))

    def own_copy(self, chunk):
        pc = self.pc
        return pltpu.make_async_copy(self.own_rows(pc.zl, chunk), self.rows(pc.f * pc.sz.ctx + pc.c, chunk),
                                     self.sems.at[chunk, 0, 0, 0])

    def along_fsdp(self, jump, step, chunk):
        pc, sz = self.pc, self.pc.sz
        rows = self.rows(pc.f * sz.ctx + pc.ctx_back(step), chunk)
        return send(rows, rows, self.sems.at[chunk, jump, 0, step], self.sems.at[chunk, jump, 1, step],
                    ((pc.f + jump) % sz.fsdp, pc.c, pc.t))

    def to_twin(self, jump, step, chunk):
        pc, sz = self.pc, self.pc.sz
        rows = self.rows((pc.f + sz.fsdp - jump) % sz.fsdp * sz.ctx + pc.ctx_back(step), chunk)
        return send(rows, rows, self.twin_sems.at[chunk, jump, 0, step], self.twin_sems.at[chunk, jump, 1, step],
                    pc.twin)

    def depart(self, chunk):
        if chunk < self.pc.sz.chunks:
            self.own_copy(chunk).start()
            for step in range(self.pc.sz.ctx - 1, 0, -1):
                self.along_ctx(step, chunk).start()

    def turn(self, chunk):
        if chunk < self.pc.sz.chunks:
            for step in range(self.pc.sz.ctx):
                self.along_ctx(step, chunk).wait_recv() if step else self.own_copy(chunk).wait()
                for jump in range(1, self.pc.sz.fsdp):
                    self.along_fsdp(jump, step, chunk).start()
                self.to_twin(0, step, chunk).start()

    def land(self, chunk):
        if chunk < self.pc.sz.chunks:
            for step in range(self.pc.sz.ctx):
                for jump in range(1, self.pc.sz.fsdp):
                    self.along_fsdp(jump, step, chunk).wait_recv()
                    self.to_twin(jump, step, chunk).start()

    def jobs(self, parts):
        calls = {"d": self.depart, "t": self.turn, "l": self.land}
        return [functools.partial(calls[part[0]], int(part[1])) for part in parts.split()]

    def run(self, parts):
        for job in self.jobs(parts):
            job()

    def finish(self):
        sz = self.pc.sz
        for chunk in range(sz.chunks):
            for step in range(sz.ctx):
                if step:
                    self.along_ctx(step, chunk).wait_send()
                for jump in range(sz.fsdp):
                    if jump:
                        self.along_fsdp(jump, step, chunk).wait_send()
                    self.to_twin(jump, step, chunk).wait()


class Give:
    def __init__(self, pc, dw, recv, got, sems, first=0):
        self.lanes = pl.ds(first, recv.shape[-1])
        self.pc, self.dw, self.recv, self.got, self.sems = pc, dw, recv, got, sems
        self.order = list(range(pc.sz.ctx - 1, -1, -1))

    def rows(self, group, chunk):
        sz = self.pc.sz
        return pl.ds(pl.multiple_of(group * sz.wrowsp + chunk * sz.chunk, 16), sz.chunk)

    def part(self, chunk):
        return pl.ds(chunk * self.pc.sz.chunk, self.pc.sz.chunk)

    def along_fsdp(self, jump, step, chunk):
        pc, sz = self.pc, self.pc.sz
        f = (pc.f + jump) % sz.fsdp
        return send(self.dw.at[self.rows(f * sz.ctx + pc.ctx_ahead(step), chunk), self.lanes],
                    self.got.at[jump - 1, step, self.part(chunk)],
                    self.sems.at[chunk, jump, 0, step], self.sems.at[chunk, jump, 1, step], (f, pc.c, pc.t))

    def along_ctx(self, step, chunk, back=False):
        pc = self.pc
        there = pc.ctx_back(step) if back else pc.ctx_ahead(step)
        return send(self.got.at[0, step, self.part(chunk)],
                    self.recv.at[pc.ctx_back(step) if back else pc.c, self.part(chunk)],
                    self.sems.at[chunk, 0, 0, step], self.sems.at[chunk, 0, 1, step], (pc.f, there, pc.t))

    def own_copy(self, chunk):
        return pltpu.make_async_copy(self.got.at[0, 0, self.part(chunk)], self.recv.at[self.pc.c, self.part(chunk)],
                                     self.sems.at[chunk, 0, 0, 0])

    def depart(self, chunk):
        if chunk < self.pc.sz.chunks:
            for step in self.order:
                for jump in range(1, self.pc.sz.fsdp):
                    self.along_fsdp(jump, step, chunk).start()

    def turn(self, chunk):
        pc, sz = self.pc, self.pc.sz
        if chunk >= sz.chunks:
            return
        for step in self.order:
            for jump in range(1, sz.fsdp):
                self.along_fsdp(jump, step, chunk).wait_recv()
            total = self.dw[self.rows(pc.f * sz.ctx + pc.ctx_ahead(step), chunk), self.lanes].astype(f32)
            for jump in range(1, sz.fsdp):
                total = total + self.got[jump - 1, step, self.part(chunk)].astype(f32)
            self.got[0, step, self.part(chunk)] = total.astype(bf16)
            self.along_ctx(step, chunk).start() if step else self.own_copy(chunk).start()

    def jobs(self, parts):
        calls = {"d": self.depart, "t": self.turn}
        return [functools.partial(calls[part[0]], int(part[1])) for part in parts.split()]

    def run(self, parts):
        for job in self.jobs(parts):
            job()

    def finish(self):
        sz = self.pc.sz
        for chunk in range(sz.chunks):
            self.own_copy(chunk).wait()
            for step in range(sz.ctx):
                if step:
                    self.along_ctx(step, chunk, True).wait_recv()
                    self.along_ctx(step, chunk).wait_send()
                for jump in range(1, sz.fsdp):
                    self.along_fsdp(jump, step, chunk).wait_send()


def chosen(sz, group, lanes_shape):
    row = lax.broadcasted_iota(jnp.int32, lanes_shape, 0)
    col = lax.broadcasted_iota(jnp.int32, lanes_shape, 1)
    return jnp.where((row - group * sz.wrows == col) & (col < sz.wrows), 1.0, 0.0).astype(bf16)


def drop_padding(sz, src, dst):
    for at in range(0, dst.shape[-1], 128):
        lanes = slice(at, at + 128)

        def step(group, total):
            rows = pl.ds(pl.multiple_of(group * sz.wrowsp, 16), sz.wrowsp)
            return total + dot(chosen(sz, group, (sz.d, sz.wrowsp)), src[rows, lanes], (1, 0))

        dst[:, lanes] = lax.fori_loop(0, sz.groups, step, jnp.zeros((sz.d, 128), f32)).astype(bf16)


def add_padding(sz, src, dst):
    def step(group, carry):
        rows = pl.ds(pl.multiple_of(group * sz.wrowsp, 16), sz.wrowsp)
        for at in range(0, dst.shape[-1], 128):
            lanes = slice(at, at + 128)
            dst[rows, lanes] = dot(chosen(sz, group, (sz.d, sz.wrowsp)), src[:, lanes], (0, 0)).astype(bf16)
        return carry

    lax.fori_loop(0, sz.groups, step, 0)


def by_unit(sz, values):
    return jnp.swapaxes(values, 0, 1).reshape(sz.half, values.shape[-1])


def shift_lanes(values, start, count, at, width):
    have = values.shape[-1]
    first, last = start // 128 * 128, up_to(start + count, 128)
    to = at // 128 * 128
    span = max(last - first, up_to(at + count, 128) - to)
    piece = values[:, first:min(last, have)].astype(f32)
    if piece.shape[-1] < span:
        piece = jnp.pad(piece, ((0, 0), (0, span - piece.shape[-1])))
    turn = ((at - to) - (start - first)) % span
    if turn:
        piece = pltpu.roll(piece, turn, 1)
    lanes = lanes_of(piece.shape)
    piece = jnp.where((lanes >= at - to) & (lanes < at - to + count), piece, 0.0)
    piece = piece[:, 0:min(span, width - to)]
    return jnp.pad(piece, ((0, 0), (to, width - to - piece.shape[-1])))


def by_rows(sz, step):
    if sz.wrows % 16:
        step(slice(0, sz.wrows))
    else:

        def one(i, carry):
            step(pl.ds(pl.multiple_of(i * 16, 16), 16))
            return carry

        lax.fori_loop(0, sz.wrows // 16, one, 0)


def half_of(pc, values, count, width, at=0):
    out = shift_lanes(values, 0, count, at, width)
    for j in range(1, pc.sz.zl):
        out = jnp.where(pc.zl == j, shift_lanes(values, j * count, count, at, width), out)
    return out


def piece_of(pc, values):
    sz = pc.sz
    values = values.astype(f32)
    over = sz.tp * sz.part - sz.rows
    if over:
        values = jnp.concatenate([values, jnp.zeros((over, sz.d), f32)], axis=0)
    out = values[0:sz.part]
    for t in range(1, sz.tp):
        out = jnp.where(pc.t == t, values[t * sz.part:(t + 1) * sz.part], out)
    return out


def steps_below(values, unit, count):
    out = jnp.zeros_like(values)
    for m in range(1, count):
        out = out + jnp.where(values >= m * unit, 1, 0)
    return out


def key_valid(pc, count):
    sz = pc.sz
    row = lax.broadcasted_iota(jnp.int32, (1, sz.keys), 1)
    core = steps_below(row, sz.half, 2)
    within = row - core * sz.half
    unit = steps_below(within, sz.part, sz.units)
    piece = steps_below(unit, sz.chips, sz.images)
    chip = unit - piece * sz.chips
    zl = steps_below(chip, sz.chips_y, sz.zl)
    t = 2 * (chip - zl * sz.chips_y) + core
    token = t * sz.part + within - unit * sz.part
    position = (piece * sz.zl + zl) * sz.rows + token
    return jnp.where((token < sz.rows) & (position < count), 1.0, 0.0)


def own_valid(pc, count):
    sz = pc.sz
    shape = (sz.images, sz.part, 1)
    piece = lax.broadcasted_iota(jnp.int32, shape, 0)
    token = pc.t * sz.part + lax.broadcasted_iota(jnp.int32, shape, 1)
    position = (piece * sz.zl + pc.zl) * sz.rows + token
    return jnp.where((token < sz.rows) & (position < count), 1.0, 0.0)


def ff_lanes(sz, values):
    lanes = lanes_of(values.shape)
    return jnp.where((lanes >= sz.ff_at) & (lanes < sz.ff_at + sz.ff), values, 0.0)


def ride(sz, src, dst, src_at, dst_at):
    def step(i, carry):
        rows = pl.ds(pl.multiple_of(i * 128, 128), 128)
        there = src[rows, src_at:src_at + 128].astype(f32)
        here = dst[rows, dst_at:dst_at + 128].astype(f32) if dst_at else jnp.zeros_like(there)
        dst[rows, dst_at:dst_at + 128] = jnp.where(lanes_of(there.shape) >= sz.ff_at, there, here).astype(bf16)
        return carry

    if sz.spare:
        lax.fori_loop(0, src.shape[0] // 128, step, 0)


def rows_of(ref, units):
    return jnp.concatenate([ref[unit] for unit in units], axis=0)


def put_rows(sz, ref, units, values):
    for i, unit in enumerate(units):
        ref[unit] = values[i * sz.part:(i + 1) * sz.part]


def attn_forward(pc, jobs, gather, w_ref, qv_ref, valid_ref, q_ref, k_ref, v_ref, mixed_ref, o_ref, kv_sems,
                 scatter):
    sz = pc.sz
    for s in range(2):
        unpack_out(sz, w_ref.at[s], o_ref.at[s])

    def project(step, carry):
        units, tokens = gather.ready(step)

        def shard(s, none):
            both3 = dot(tokens, w_ref[s, :, 0:sz.qkvp], (1, 0))
            put_rows(sz, q_ref.at[s], units, (take(sz, both3, 0) + qv_ref[s, 0:1, 0:sz.headp]).astype(bf16))
            put_rows(sz, k_ref.at[s, pc.k], units, take(sz, both3, 1).astype(bf16))
            put_rows(sz, v_ref.at[s, pc.k], units, (take(sz, both3, 2) + qv_ref[s, 1:2, 0:sz.headp]).astype(bf16))
            return none

        lax.fori_loop(0, 2, shard, 0)
        jobs.at("project", step)
        return carry

    def swaps(piece):
        units = pl.ds(piece * sz.chips, sz.chips)
        return [Swap(pc, ref.at[s, pc.k, units], ref.at[s, pc.k, units], kv_sems.at[0, i, s, piece],
                     kv_sems.at[1, i, s, piece]) for s in range(2) for i, ref in enumerate((k_ref, v_ref))]

    per = sz.steps // sz.images
    for piece in range(sz.images):
        lax.fori_loop(piece * per, (piece + 1) * per, project, 0)
        for swap in swaps(piece):
            swap.start()
    gather.finish()
    for piece in range(sz.images):
        for swap in swaps(piece):
            swap.wait()

    def attend(step, carry):
        units = scatter.units(step)

        def shard(s, partial):
            keys = k_ref[s].reshape(sz.keys, sz.headp)
            values = v_ref[s].reshape(sz.keys, sz.headp)
            queries = rows_of(q_ref.at[s], units)
            total = jnp.zeros((sz.tile, sz.headp), f32)
            for head in range(sz.heads):
                probs = probabilities(head_of(queries, head), keys, valid_ref[...])
                total = total + dot(probs.astype(bf16), head_of(values, head), (1, 0))
            mixed = total.astype(bf16)
            put_rows(sz, mixed_ref.at[s], units, mixed)
            return partial + dot(mixed, o_ref[s], (1, 1))

        partial = lax.fori_loop(0, 2, shard, jnp.zeros((sz.tile, sz.d), f32))
        scatter.push(step, partial)
        jobs.at("attend", step)
        return carry

    lax.fori_loop(0, sz.steps, attend, 0)
    jobs.run("turnover")
    scatter.flush()
    jobs.run("flush")


def ff_forward(pc, jobs, gather, w_ref, upb_ref, pre_ref, hidden_ref, scatter):
    sz = pc.sz

    def feed(step, carry):
        units, tokens = gather.ready(step)

        def shard(s, partial):
            pre = dot(tokens, w_ref[s, :, 0:sz.ffp], (1, 0)) + upb_ref[s, 2:3, 0:sz.ffp]
            put_rows(sz, pre_ref.at[s], units, pre)
            hidden = 0.5 * pre * (1.0 + jnp.tanh(gelu_root * (pre + gelu_cubic * pre * pre * pre)))
            hidden = ff_lanes(sz, hidden)
            if sz.down_shift != sz.ff_at:
                hidden = pltpu.roll(hidden, (sz.down_shift - sz.ff_at) % sz.ffp, 1)
            hidden = hidden.astype(bf16)
            put_rows(sz, hidden_ref.at[s], units, hidden)
            return partial + dot(hidden, w_ref[s, :, sz.down_at:], (1, 1))

        partial = lax.fori_loop(0, 2, shard, jnp.zeros((sz.tile, sz.d), f32))
        scatter.push(step, partial)
        jobs.at("feed", step)
        return carry

    lax.fori_loop(0, sz.steps, feed, 0)
    jobs.run("flush")
    gather.finish()


def plan(steps, more_steps, flush, what, ff, attn):
    for place, ff_parts, attn_parts in what:
        jobs = (ff.jobs(ff_parts) if ff else []) + (attn.jobs(attn_parts) if attn else [])
        if place == "f":
            flush.extend(jobs)
        else:
            table = steps if place[0] == "s" else more_steps
            table[int(place[1])] = table.get(int(place[1]), []) + jobs


def planned(what, give):
    steps = {}
    plan(steps, None, None, what, give, None)
    return steps


GIVE_FF = (("s0", "", "t0"), ("s1", "", "d2 t1"), ("s3", "", "t2"))
GIVE_ATTN = (("s0", "t0", ""), ("s1", "d2", ""), ("s2", "t1", ""), ("s3", "t2", ""))
PLAN_ATTN_FIRST = (("s0", "d2", ""), ("s3", "t1", ""), ("m0", "l0", ""), ("m1", "", "d0"), ("m2", "t2 l1", ""),
                   ("m3", "", "d1"), ("f", "l2", "d2 t0"))
PLAN_ATTN = (("s1", "t1", "d0"), ("s2", "d2", ""), ("s3", "l0", ""), ("m0", "", "d1"), ("m1", "t2 l1", ""),
             ("m3", "", "d2"), ("f", "l2", "t0"))
PLAN_FF = (("s0", "d0", "t1 l0"), ("s1", "d1", "t2"), ("s2", "t0", "l1"), ("s3", "", "l2"))


def norm_low(values, gain, shift):
    high, _ = normalised(values)
    return (high * gain + shift).astype(bf16)


def forward_kernel(sz, *refs):
    n = sz.layers
    aligned = sz.wrowsp == sz.wrows
    ins, outs, scratch = refs[:12], refs[12:12 + 13 * n + 1], refs[12 + 13 * n + 1:]
    (count_ref, in_ref, cot_ref, wqkv_ref, wout_ref, wup_ref, wdown_ref, gain_ref, shift_ref, qv_ref, upb_ref,
     resid_ref) = ins
    saved, (wattn_outs, wff_outs, ends_ref) = outs[:11 * n], split_refs(outs[11 * n:], n, n, 1)
    saved = [saved[l * 11:(l + 1) * 11] for l in range(n)]
    ends_ref = ends_ref[0]
    (own_attn, own_ff, all_attn, all_ff, swap_ref, mine_ref, n_ref, q_ref, k_ref, v_ref, mixed_ref, pre_ref,
     hidden_ref, stream_ref, middle_ref, valid_ref, o_ref, bias_ref, tsems, csems, wsems, vsems, kv_sems,
     bsems), team, joined = split_refs(scratch, 24, 6, 0 if aligned else 2)
    bufs, (gsems, ssems) = team[:4], team[4:]
    pc = Place(sz)
    greeting = Greeting(team_peers(pc) + weight_peers(pc, True))

    def pack(ref, pieces):
        def step(rows):
            total = None
            for values, start, count, at in pieces:
                piece = shift_lanes(values[rows, :], start, count, at, ref.shape[-1])
                total = piece if total is None else total + piece
            ref[rows, :] = total.astype(bf16)

        by_rows(sz, step)
        if not aligned:
            ref[sz.wrows:, :] = jnp.zeros((sz.wrowsp - sz.wrows, ref.shape[-1]), bf16)

    def pack_attn(layer):
        for half in range(sz.zl):
            pieces = [(wqkv_ref.at[layer, kind], half * sz.wide, sz.wide, kind * sz.wide) for kind in range(3)]
            pieces += [(wout_ref.at[layer], half * sz.wide, sz.wide, 3 * sz.wide)]
            if sz.spare:
                pieces += [(wup_ref.at[layer], half * sz.ff, sz.spare, 4 * sz.wide)]
            pack(own_attn.at[layer, half], pieces)

    def pack_ff(layer):
        for half in range(sz.zl):
            rest = sz.ff - sz.spare
            pack(own_ff.at[layer, half], [(wup_ref.at[layer], half * sz.ff + sz.spare, rest, 0),
                                          (wdown_ref.at[layer], half * sz.ff, sz.ff, rest)])

    for image in range(sz.images):
        swap_ref[image, 0] = piece_of(pc, in_ref[image]).astype(bf16)
        swap_ref[image, 1] = piece_of(pc, cot_ref[image]).astype(bf16)
    pack_attn(0)
    attn = [Fetch(pc, own_attn.at[l], all_attn.at[l], wsems.at[2 * l], vsems.at[2 * l]) for l in range(n)]
    ff = [Fetch(pc, own_ff.at[l], all_ff.at[l], wsems.at[2 * l + 1], vsems.at[2 * l + 1], sz.ff_sent)
          for l in range(n)]
    bias_ref[:, pc.k] = jnp.zeros((n, 8, bias_ref.shape[-1]), f32)
    for l in range(n):
        bias_ref[l, pc.k, 0:2, 0:sz.headp] = half_of(pc, qv_ref[l], sz.wide, sz.headp)
        bias_ref[l, pc.k, 2:3, 0:sz.ffp] = half_of(pc, upb_ref[l:l + 1, :], sz.ff, sz.ffp, sz.ff_at)
    bias_swaps = [Swap(pc, bias_ref.at[l, pc.k], bias_ref.at[l, pc.k], bsems.at[0, l], bsems.at[1, l])
                  for l in range(n)]
    copies = Copies(csems)

    def swap(step):
        zh = (pc.zh + step) % sz.images
        return send(swap_ref.at[zh], mine_ref.at[pc.zh], tsems.at[0, step], tsems.at[1, step],
                    (pc.f, zh * sz.zl + pc.zl, pc.t))

    greeting.wait()
    for step in range(1, sz.images):
        swap(step).start()
    attn[0].run("d0 d1 d2")
    for move in bias_swaps:
        move.start()
    mine_ref[pc.zh] = swap_ref[pc.zh]
    count = count_ref[pc.zh]
    valid_ref[...] = key_valid(pc, count)
    for step in range(1, sz.images):
        swap(step).wait()
    stream_ref[0] = mine_ref[:, 0].astype(f32)
    gathers = [Gather(pc, n_ref.at[i], gsems.at[i], FORWARD_TURN[i % 2]) for i in range(2 * n)]
    scatters = [Scatter(pc, bufs, ssems.at[i], i % 2 == 0, i % 2 == 0 and SUM_TURN[0]) for i in range(2 * n)]
    for p in range(sz.images):
        gathers[0].start(p, norm_low(stream_ref[0, p], gain_ref[0, 0:1, :], shift_ref[0, 0:1, :]))
    pack_ff(0)
    attn[0].run("t0")
    ff[0].run("d0")
    for layer in range(1, n):
        pack_attn(layer)
    attn[0].run("t1")
    ff[0].run("d1")
    ends_ref[...] = mine_ref[:, 1].astype(f32) * own_valid(pc, count)
    attn[0].run("l0 t2")
    for layer in range(1, n):
        pack_ff(layer)
    attn[0].run("l1")
    ff[0].run("t0")
    attn[0].run("l2")
    for move in bias_swaps:
        move.wait()
    attn[0].finish()

    def ready(fetch, refs, kind, layer, out):
        ref = refs.at[layer]
        if not aligned:
            for s in range(2):
                drop_padding(sz, ref.at[s], joined[kind].at[s])
            ref = joined[kind]
            pltpu.sync_copy(ref, out)
        else:
            copies.start(ref, out)
        return ref

    def after_attn(l, p):
        def run():
            middle = stream_ref[l, p] + (scatters[2 * l].finish(p) + resid_ref[l, 0:1, :])
            middle_ref[l, p] = middle
            gathers[2 * l + 1].start(p, norm_low(middle, gain_ref[l, 1:2, :], shift_ref[l, 1:2, :]))

        return run

    def after_ff(l, p):
        def run():
            out = middle_ref[l, p] + (scatters[2 * l + 1].finish(p) + resid_ref[l, 1:2, :])
            stream_ref[l + 1, p] = out
            if l + 1 < n:
                gathers[2 * l + 2].start(p, norm_low(out, gain_ref[l + 1, 0:1, :], shift_ref[l + 1, 0:1, :]))

        return run

    per = sz.steps // sz.images
    rest = range(1, sz.images)
    for l in range(n):
        more = l + 1 < n
        w = ready(attn[l], all_attn, 0, l, wattn_outs[l])
        project = {p * per - 1: [after_ff(l - 1, p)] for p in rest} if l else {}
        attend, flush = {}, []
        plan(project, attend, flush, PLAN_ATTN_FIRST if l == 0 else PLAN_ATTN, ff[l], attn[l + 1] if more else None)
        jobs = Jobs(project=project, attend=attend, flush=flush, turnover=[after_attn(l, 0)])
        attn_forward(pc, jobs, gathers[2 * l], w, bias_ref.at[l], valid_ref, q_ref.at[l], k_ref.at[l], v_ref.at[l],
                     mixed_ref.at[l], o_ref, kv_sems.at[l], scatters[2 * l])
        for ref, to in ((stream_ref.at[l], 0), (n_ref.at[2 * l], 2), (q_ref.at[l], 4), (k_ref.at[l], 5),
                        (v_ref.at[l], 6), (mixed_ref.at[l], 7)):
            copies.start(ref, saved[l][to])
        ff[l].finish()
        for core in range(2):
            ride(sz, all_attn.at[l, core], all_ff.at[l, core], 4 * sz.wide - sz.ff_at, 0)
        w = ready(ff[l], all_ff, 1, l, wff_outs[l])
        feed = {(p - 1) * per: [after_attn(l, p)] for p in rest}
        if more:
            plan(feed, None, None, PLAN_FF, ff[l + 1], attn[l + 1])
        feed[FF_OVER] = [after_ff(l, 0)] + feed.get(FF_OVER, [])
        ff_forward(pc, Jobs(feed=feed), gathers[2 * l + 1], w, bias_ref.at[l], pre_ref.at[l],
                   hidden_ref.at[l], scatters[2 * l + 1])
        if more:
            attn[l + 1].finish()
        else:
            for p in rest:
                after_ff(l, p)()
        for ref, to in ((middle_ref.at[l], 1), (n_ref.at[2 * l + 1], 3), (pre_ref.at[l], 8), (hidden_ref.at[l], 9)):
            copies.start(ref, saved[l][to])
    copies.start(stream_ref.at[n], saved[0][10])
    copies.start(valid_ref, saved[n - 1][10])
    copies.wait()


def forward_call(sz, *operands):
    n = sz.layers
    own, team = ((sz.images, sz.part, sz.d), f32), ((sz.chips, sz.images, sz.part, sz.d), bf16)
    head, pair = (2, sz.units, sz.part, sz.headp), (2, 2, sz.units, sz.part, sz.headp)
    hidden = (2, sz.units, sz.part, sz.ffp)
    shapes = []
    for l in range(n):
        last = ((1, sz.keys), f32) if l == n - 1 else own
        shapes += [own, own, team, team, (head, bf16), (pair, bf16), (pair, bf16), (head, bf16), (hidden, f32),
                   (hidden, bf16), last]
    shapes += [((2, sz.d, sz.attnp), bf16)] * n + [((2, sz.d, sz.ffw), bf16)] * n + [own]
    vmem, hbm = pl.BlockSpec(memory_space=pltpu.VMEM), pl.BlockSpec(memory_space=pl.ANY)
    padded = sz.groups * sz.wrowsp
    scratch = [
        VMEM((n, sz.zl, sz.wrowsp, sz.attnp), bf16), VMEM((n, sz.zl, sz.wrowsp, sz.ffs), bf16),
        VMEM((n, 2, padded, sz.attnp), bf16), VMEM((n, 2, padded, sz.ffw), bf16),
        VMEM((sz.images, 2, sz.part, sz.d), bf16), VMEM((sz.images, 2, sz.part, sz.d), bf16),
        VMEM((2 * n,) + team[0], bf16),
        VMEM((n,) + head, bf16), VMEM((n,) + pair, bf16), VMEM((n,) + pair, bf16), VMEM((n,) + head, bf16),
        VMEM((n,) + hidden, f32), VMEM((n,) + hidden, bf16),
        VMEM((n + 1,) + own[0], f32), VMEM((n,) + own[0], f32), VMEM((1, sz.keys), f32),
        VMEM((2, sz.d, sz.headp), bf16), VMEM((n, 2, 8, max(sz.headp, sz.ffp)), f32),
        DMA((2, sz.images)), DMA((12 * n + 2,)), DMA((2 * n, sz.chunks, sz.fsdp, 2, sz.ctx)),
        DMA((2 * n, sz.chunks, sz.fsdp, 2, sz.ctx)), DMA((n, 2, 2, 2, sz.images)), DMA((2, n)),
    ] + team_scratch(sz, 2 * n)
    if sz.wrowsp != sz.wrows:
        scratch += [VMEM((2, sz.d, sz.attnp), bf16), VMEM((2, sz.d, sz.ffw), bf16)]
    return pl.pallas_call(
        functools.partial(forward_kernel, sz),
        out_shape=[jax.ShapeDtypeStruct(*s) for s in shapes],
        in_specs=[pl.BlockSpec(memory_space=pltpu.SMEM)] + [vmem] * (len(operands) - 1),
        out_specs=[hbm] * (len(shapes) - 1) + [vmem],
        scratch_shapes=scratch,
        compiler_params=params(1),
        name="forward",
    )(*operands)


def params(collective_id):
    return pltpu.CompilerParams(
        collective_id=collective_id, has_side_effects=True, vmem_limit_bytes=63 * 1024 * 1024
    )


class Twins:
    def __init__(self, pc, dw, got, sems, span):
        self.pc, self.dw, self.got, self.sems, self.span = pc, dw, got, sems, span
        self.count = pc.sz.d // span

    def copy(self, i):
        rows = pl.ds(pl.multiple_of(i * self.span, 128), self.span)
        return send(self.dw.at[1 - self.pc.k, rows], self.got.at[rows], self.sems.at[0, i], self.sems.at[1, i],
                    self.pc.twin)

    def put(self, core, i, pieces):
        rows = pl.ds(pl.multiple_of(i * self.span, 128), self.span)
        for at, values in pieces:
            self.dw[core, rows, at:at + values.shape[-1]] = values.astype(bf16)

    def run(self, make, jobs, between=None):
        def other(i, carry):
            self.put(1 - self.pc.k, i, make(1 - self.pc.k, i))
            self.copy(i).start()
            return carry

        def own(i, carry):
            self.put(self.pc.k, i, make(self.pc.k, i))
            jobs.at("step_grads", i)
            return carry

        def add(i, carry):
            self.copy(i).wait_recv()
            rows = pl.ds(pl.multiple_of(i * self.span, 128), self.span)
            self.dw[self.pc.k, rows, :] = (
                self.dw[self.pc.k, rows, :].astype(f32) + self.got[rows, :].astype(f32)
            ).astype(bf16)
            self.copy(i).wait_send()
            return carry

        lax.fori_loop(0, self.count, other, 0)
        if between:
            between()
        lax.fori_loop(0, self.count, own, 0)
        lax.fori_loop(0, self.count, add, 0)


def ff_backward(pc, jobs, gather, w_ref, n2_ref, pre_ref, hidden_ref, dup_ref, pg_ref, twins, scatter):
    sz = pc.sz
    dup_ref[...] = jnp.zeros_like(dup_ref)

    def feed(step, carry):
        units, tokens = gather.ready(step)

        def shard(s, partial):
            back = dot(tokens, w_ref[s, :, sz.down_at:], (1, 0))
            if sz.down_shift != sz.ff_at:
                back = pltpu.roll(back, (sz.ff_at - sz.down_shift) % sz.ffp, 1)
            pre = rows_of(pre_ref.at[s], units)
            bent = jnp.tanh(gelu_root * (pre + gelu_cubic * pre * pre * pre))
            slope = 0.5 * (1.0 + bent) + 0.5 * pre * (1.0 - bent * bent) * (
                gelu_root * (1.0 + 3.0 * gelu_cubic * pre * pre)
            )
            pre_grad = ff_lanes(sz, back * slope).astype(bf16)
            put_rows(sz, pg_ref.at[s], units, pre_grad)
            dup_ref[s] += jnp.sum(pre_grad.astype(f32), axis=0, keepdims=True)
            return partial + dot(pre_grad, w_ref[s, :, 0:sz.ffp], (1, 1))

        partial = lax.fori_loop(0, 2, shard, jnp.zeros((sz.tile, sz.d), f32))
        scatter.push(step, partial)
        jobs.at("feed", step)
        return carry

    lax.fori_loop(0, sz.steps, feed, 0)
    jobs.run("flush")

    def make(core, i):
        lanes = pl.ds(pl.multiple_of(i * twins.span, 128), twins.span)
        hidden = hidden_ref[core].reshape(sz.half, sz.ffp)
        down = dot(by_unit(sz, gather.buf[:, :, :, lanes]), hidden, (0, 0))
        pre_grad = pg_ref[core].reshape(sz.half, sz.ffp)
        up = dot(by_unit(sz, n2_ref[:, :, :, lanes]), pre_grad, (0, 0))
        over = sz.ffp - sz.down_at
        both = [(sz.down_at, up[:, sz.down_at:] + down[:, 0:over])] if over else []
        return [(0, up[:, 0:sz.down_at])] + both + [(sz.ffp, down[:, over:])]

    twins.run(make, jobs)
    jobs.run("grads")
    gather.finish()


def attn_backward(pc, jobs, gather, w_ref, n1_ref, q_ref, k_ref, v_ref, mixed_ref, valid_ref, dqv_ref,
                  o_ref, dkv_ref, kvsend_ref, kvgot_ref, stack_ref, kv_sems, twins, scatter):
    sz = pc.sz
    for s in range(2):
        unpack_out(sz, w_ref.at[s], o_ref.at[s])
    dkv_ref[...] = jnp.zeros_like(dkv_ref)
    dqv_ref[...] = jnp.zeros_like(dqv_ref)
    scale = HEAD_DIM ** (-0.5)

    def attend(step, carry):
        units, tokens = gather.ready(step)

        def shard(s, none):
            mixed_grad = dot(tokens, o_ref[s], (1, 0)).astype(bf16)
            keys = k_ref[s].reshape(sz.keys, sz.headp)
            values = v_ref[s].reshape(sz.keys, sz.headp)
            queries = rows_of(q_ref.at[s], units)
            total = jnp.zeros((sz.tile, sz.headp), f32)
            dkey, dvalue = None, None
            for head in range(sz.heads):
                q_head = head_of(queries, head)
                g_head = head_of(mixed_grad, head)
                probs = probabilities(q_head, keys, valid_ref[...])
                dprobs = dot(g_head, values, (1, 1))
                inner = jnp.sum(probs * dprobs, axis=-1, keepdims=True)
                dscores = (probs * (dprobs - inner)).astype(bf16)
                total = total + dot(dscores, head_of(keys, head), (1, 0))
                dk, dv = dot(dscores, q_head, (0, 0)), dot(probs.astype(bf16), g_head, (0, 0))
                dkey = dk if dkey is None else dkey + dk
                dvalue = dv if dvalue is None else dvalue + dv
            dkv_ref[s, 0] += dkey.reshape(2, sz.half, sz.headp)
            dkv_ref[s, 1] += dvalue.reshape(2, sz.half, sz.headp)
            dq = (scale * total).astype(bf16).astype(f32)
            dqv_ref[s, 0:1, :] += jnp.sum(dq, axis=0, keepdims=True)
            dq = dq.astype(bf16)
            for i, unit in enumerate(units):
                stack_ref[s, unit, :, 0:sz.headp] = dq[i * sz.part:(i + 1) * sz.part]
            return none

        lax.fori_loop(0, 2, shard, 0)
        jobs.at("attend", step)
        return carry

    lax.fori_loop(0, sz.steps, attend, 0)
    for s in range(2):
        kvsend_ref[s] = dkv_ref[s, :, 1 - pc.k].astype(bf16)
    moves = [Swap(pc, kvsend_ref.at[s], kvgot_ref.at[s], kv_sems.at[0, s], kv_sems.at[1, s]) for s in range(2)]
    for move in moves:
        move.start()
    gather.finish()
    jobs.run("middle")
    for move in moves:
        move.wait()

    def back_project(step, carry):
        units = scatter.units(step)

        def shard(s, partial):

            def both(kind):
                rows = [pl.ds(pl.multiple_of(unit * sz.part, sz.part), sz.part) for unit in units]
                return jnp.concatenate(
                    [dkv_ref[s, kind, pc.k, r, :] + kvgot_ref[s, kind, r, :].astype(f32) for r in rows], axis=0
                )

            dk = (scale * both(0)).astype(bf16).astype(f32)
            dv = both(1).astype(bf16).astype(f32)
            dqv_ref[s, 1:2, :] += jnp.sum(dv, axis=0, keepdims=True)
            dq = rows_of(stack_ref.at[s], units)[:, 0:sz.headp].astype(f32)
            total = jnp.pad(dq, ((0, 0), (0, sz.qkvp - sz.headp)))
            for kind, piece in ((1, dk), (2, dv)):
                start = kind * sz.wide // 128 * 128
                shift = kind * sz.wide - start
                moved = pltpu.roll(piece, shift, 1) if shift else piece
                total = total + jnp.pad(moved, ((0, 0), (start, sz.qkvp - start - sz.headp)))
            stacked = total.astype(bf16)
            put_rows(sz, stack_ref.at[s], units, stacked)
            return partial + dot(stacked, w_ref[s, :, 0:sz.qkvp], (1, 1))

        partial = lax.fori_loop(0, 2, shard, jnp.zeros((sz.tile, sz.d), f32))
        scatter.push(step, partial)
        return carry

    lax.fori_loop(0, sz.steps, back_project, 0)
    jobs.run("flush")
    o_at = 3 * sz.wide // 128 * 128
    o_shift = 3 * sz.wide - o_at

    def make(core, i):
        lanes = pl.ds(pl.multiple_of(i * twins.span, 128), twins.span)
        stacked = stack_ref[core].reshape(sz.half, sz.qkvp)
        dqkv = dot(by_unit(sz, n1_ref[:, :, :, lanes]), stacked, (0, 0))
        mixed = mixed_ref[core].reshape(sz.half, sz.headp)
        dout = dot(by_unit(sz, gather.buf[:, :, :, lanes]), mixed, (0, 0))
        if o_shift:
            dout = pltpu.roll(dout, o_shift, 1)
        total = jnp.pad(dqkv, ((0, 0), (0, sz.attnp - sz.qkvp))) + jnp.pad(
            dout, ((0, 0), (o_at, sz.attnp - o_at - sz.headp))
        )
        return [(0, total)]

    twins.run(make, jobs, scatter.flush)
    jobs.run("grads")


def backward_kernel(sz, *refs):
    n = sz.layers
    aligned = sz.wrowsp == sz.wrows
    saved = [refs[l * 11:(l + 1) * 11] for l in range(n)]
    wattn_ins, wff_ins, (cot_ref, gain_ref), outs, scratch = split_refs(
        refs[11 * n:], n, n, 2, 2 * n + 2, len(refs) - 11 * n - 2 * n - 2 - 2 * n - 2)
    attn_outs, ff_outs, (whole_ref, small_ref) = split_refs(outs, n, n, 2)
    (stream_ref, middle_ref, n1_ref, n2_ref, q_ref, k_ref, v_ref, mixed_ref, pre_ref, hidden_ref, valid_ref, out_ref,
     wattn_ref, wff_ref, gl_ref, ml_ref, pg_ref, o_ref, dkv_ref, kvsend_ref, kvgot_ref, stack_ref, dwattn_ref,
     dwff_ref, twattn_ref, twff_ref, got_attn, got_ff, dqv_ref, dup_ref, grad_ref, ends_ref, first, from_tp, from_ctx,
     from_fsdp, sum_tp, sum_ctx, share_ref, shgot_ref, lsems, wsems, esems, ysems, tsems, kv_sems, twsems,
     shsems), team, padded = split_refs(scratch, 48, 6, 0 if aligned else 2)
    bufs, (gsems, ssems) = team[:4], team[4:]
    pc = Place(sz)
    greeting = Greeting(team_peers(pc) + weight_peers(pc, True) + line_peers(pc))
    copies = Copies(lsems)
    into = [stream_ref, middle_ref, n1_ref, n2_ref, q_ref, k_ref, v_ref, mixed_ref, pre_ref, hidden_ref]

    def load(l, weights, ref, kinds):
        return [copies.start(weights[l], ref)] + [copies.start(saved[l][kind], into[kind]) for kind in kinds]

    def load_ff(l):
        return load(l, wff_ins, wff_ref, (8, 3, 9, 1))

    def load_attn(l):
        return load(l, wattn_ins, wattn_ref, (4, 5, 6, 7, 2, 0))

    out_load = copies.start(saved[0][10], out_ref)
    ff_loads, attn_loads = load_ff(n - 1), load_attn(n - 1)
    attn_loads.append(copies.start(saved[n - 1][10], valid_ref))
    own_attn, own_ff = dwattn_ref.at[pc.k], dwff_ref.at[pc.k]
    give_attn = [Give(pc, own_attn if aligned else padded[0], attn_outs[l], got_attn.at[l], wsems.at[2 * l])
                 for l in range(n)]
    give_ff = [Give(pc, own_ff if aligned else padded[1], ff_outs[l], got_ff.at[l], wsems.at[2 * l + 1], sz.ff_sent)
               for l in range(n)]

    def begin(give, dw, kind):
        def run():
            if kind == 0:
                ride(sz, own_ff, dw, 0, 4 * sz.wide - sz.ff_at)
            if not aligned:
                add_padding(sz, dw, padded[kind])
            give.run("d0 d1")

        return run

    def swap(kind, step):
        zh = (pc.zh + step) % sz.images
        return send(ends_ref.at[kind, zh], whole_ref.at[kind, pc.t, pc.zh], esems.at[kind, 0, step],
                    esems.at[kind, 1, step], (pc.f, zh * sz.zl + pc.zl, pc.t))

    def own_end(kind):
        return pltpu.make_async_copy(ends_ref.at[kind, pc.zh], whole_ref.at[kind, pc.t, pc.zh], esems.at[kind, 0, 0])

    def spread(kind, step):
        return send(whole_ref.at[kind, pc.t], whole_ref.at[kind, pc.t], ysems.at[kind, 0, step],
                    ysems.at[kind, 1, step], (pc.f, pc.c, (pc.t + step) % sz.tp))

    def spread_from(kind, step):
        back = (pc.t + sz.tp - step) % sz.tp
        return send(whole_ref.at[kind, back], whole_ref.at[kind, back], ysems.at[kind, 0, step],
                    ysems.at[kind, 1, step], (pc.f, pc.c, back))

    def swap_start(kind):
        own_end(kind).start()
        for step in range(1, sz.images):
            swap(kind, step).start()

    def spread_start(kind):
        own_end(kind).wait()
        for step in range(1, sz.images):
            swap(kind, step).wait()
        for step in range(1, sz.tp):
            spread(kind, step).start()

    def spread_wait(kind):
        for step in range(1, sz.tp):
            spread_from(kind, step).wait_recv()
            spread(kind, step).wait_send()

    def over_tp(step):
        return send(first, from_tp.at[step - 1], tsems.at[0, 0, step], tsems.at[0, 1, step],
                    (pc.f, pc.c, (pc.t + step) % sz.tp))

    def over_ctx(step):
        return send(sum_tp, from_ctx.at[step - 1], tsems.at[1, 0, step], tsems.at[1, 1, step],
                    (pc.f, pc.ctx_ahead(step), pc.t))

    def over_fsdp(step):
        return send(sum_ctx, from_fsdp.at[step - 1], tsems.at[2, 0, step], tsems.at[2, 1, step],
                    ((pc.f + step) % sz.fsdp, pc.c, pc.t))

    sum_tp[...] = jnp.zeros_like(sum_tp)
    share_ref[...] = jnp.zeros_like(share_ref)
    first[...] = jnp.zeros_like(first)
    copies.wait([out_load])
    ends_ref[0] = out_ref[...].astype(bf16)
    grad_ref[...] = cot_ref[...]
    gathers = [Gather(pc, (gl_ref, ml_ref)[i % 2], gsems.at[i], BACKWARD_TURN[1 - i % 2]) for i in range(2 * n)]
    scatters = [Scatter(pc, bufs, ssems.at[i], i % 2 == 1, i % 2 == 1 and SUM_TURN[1]) for i in range(2 * n)]
    def low_of(l, p, row):
        low = grad_ref[p].astype(bf16)
        first[l, row:row + 1, :] += jnp.sum(low.astype(f32), axis=0, keepdims=True)
        return low

    def after_ff(l, p):
        def run():
            turn = n - 1 - l
            term, dgain, dshift = norm_back(middle_ref[p], gain_ref[l, 1:2, :], scatters[2 * turn].finish(p))
            grad_ref[p] += term
            gathers[2 * turn + 1].start(p, low_of(l, p, 4))
            first[l, 1:2, :] += dgain
            first[l, 3:4, :] += dshift

        return run

    def after_attn(l, p):
        def run():
            turn = n - 1 - l
            term, dgain, dshift = norm_back(stream_ref[p], gain_ref[l, 0:1, :], scatters[2 * turn + 1].finish(p))
            grad_ref[p] += term
            if l:
                gathers[2 * turn + 2].start(p, low_of(l - 1, p, 5))
            else:
                ends_ref[1, p] = grad_ref[p].astype(bf16)
            first[l, 0:1, :] += dgain
            first[l, 2:3, :] += dshift

        return run

    greeting.wait()
    per, rest = sz.steps // sz.images, range(1, sz.images)
    span = 384 if sz.d % 384 == 0 else 128
    for p in range(sz.images):
        gathers[0].start(p, low_of(n - 1, p, 5))
    swap_start(0)
    for turn in range(n):
        l = n - 1 - turn
        start = turn == 0
        copies.wait(ff_loads)
        feed = {}
        if start:
            feed[1] = [lambda: spread_start(0)]
        else:
            after = give_attn[l + 1]
            feed.update({(p - 1) * per: [after_attn(l + 1, p)] for p in rest})
            feed[(sz.images - 2) * per] = feed[(sz.images - 2) * per] + [lambda: attn_loads.extend(load_attn(l))]
            plan(feed, None, None, GIVE_FF, None, after)
        feed[FF_OVER] = [after_ff(l, 0)] + feed.get(FF_OVER, [])
        jobs = Jobs(feed=feed, flush=([] if start else [give_ff[l + 1].finish]),
                    grads=[begin(give_ff[l], own_ff, 1)] + [after_ff(l, p) for p in rest])
        twins = Twins(pc, dwff_ref, twff_ref, twsems.at[2 * l + 1], span)
        ff_backward(pc, jobs, gathers[2 * turn], wff_ref, n2_ref, pre_ref, hidden_ref, dup_ref, pg_ref, twins,
                    scatters[2 * turn])
        for core in range(2):
            share_ref[core, 3 * l + 2:3 * l + 3, 0:sz.ffp] = dup_ref[core]
        copies.wait(attn_loads)
        del attn_loads[:]
        if l:
            ff_loads = load_ff(l - 1)
        if start:
            spread_wait(0)
        now = give_ff[l]
        jobs = Jobs(
            attend=planned(GIVE_ATTN, now),
            flush=([] if start else [give_attn[l + 1].finish]),
            step_grads={0: [after_attn(l, 0)]}, grads=[begin(give_attn[l], own_attn, 0)],
        )
        twins = Twins(pc, dwattn_ref, twattn_ref, twsems.at[2 * l], span)
        attn_backward(pc, jobs, gathers[2 * turn + 1], wattn_ref, n1_ref, q_ref, k_ref, v_ref, mixed_ref, valid_ref,
                      dqv_ref, o_ref, dkv_ref, kvsend_ref, kvgot_ref, stack_ref, kv_sems.at[l], twins,
                      scatters[2 * turn + 1])
        for core in range(2):
            share_ref[core, 3 * l:3 * l + 2, 0:sz.headp] = dqv_ref[core]
    share = Swap(pc, share_ref.at[1 - pc.k], shgot_ref, shsems.at[0], shsems.at[1])
    share.start()
    for p in rest:
        after_attn(0, p)()
    last = give_attn[0]
    swap_start(1)
    for step in range(1, sz.tp):
        over_tp(step).start()
    last.run("d2 t0")
    spread_start(1)
    last.run("t1")
    value = first[...]
    for step in range(1, sz.tp):
        over_tp(step).wait()
        value = value + from_tp[step - 1]
    sum_tp[0:n] = value
    share.wait()
    sum_tp[n + pc.zl] = share_ref[pc.k] + shgot_ref[...]
    for step in range(1, sz.ctx):
        over_ctx(step).start()
    last.run("t2")
    value = sum_tp[...]
    for step in range(1, sz.ctx):
        over_ctx(step).wait()
        value = value + from_ctx[step - 1]
    sum_ctx[...] = value
    for step in range(1, sz.fsdp):
        over_fsdp(step).start()
    value = sum_ctx[...]
    for step in range(1, sz.fsdp):
        over_fsdp(step).wait()
        value = value + from_fsdp[step - 1]
    small_ref[...] = value
    give_ff[0].finish()
    spread_wait(1)
    last.finish()


def backward_call(sz, saved, wattn, wff, cot, gains):
    n = sz.layers
    own, team = (sz.images, sz.part, sz.d), (sz.chips, sz.images, sz.part, sz.d)
    head, pair = (2, sz.units, sz.part, sz.headp), (2, 2, sz.units, sz.part, sz.headp)
    hidden = (2, sz.units, sz.part, sz.ffp)
    deep = up_to(max(6, 3 * n), 8)
    small = (n + sz.zl, deep, sz.d)
    ends = (sz.images, sz.part, sz.d)
    attn_sum, ff_sum = (sz.ctx, sz.wrowsp, sz.attnp), (sz.ctx, sz.wrowsp, sz.ffs)
    shapes = [(attn_sum, bf16)] * n + [(ff_sum, bf16)] * n + [((2, sz.tp) + ends, bf16), (small, f32)]
    vmem, hbm = pl.BlockSpec(memory_space=pltpu.VMEM), pl.BlockSpec(memory_space=pl.ANY)
    far, jumps = max(sz.tp, sz.ctx, sz.fsdp), max(sz.fsdp - 1, 1)
    scratch = [
        VMEM(own, f32), VMEM(own, f32), VMEM(team, bf16), VMEM(team, bf16),
        VMEM(head, bf16), VMEM(pair, bf16), VMEM(pair, bf16), VMEM(head, bf16), VMEM(hidden, f32), VMEM(hidden, bf16),
        VMEM((1, sz.keys), f32), VMEM(own, f32),
        VMEM((2, sz.d, sz.attnp), bf16), VMEM((2, sz.d, sz.ffw), bf16),
        VMEM(team, bf16), VMEM(team, bf16), VMEM(hidden, bf16), VMEM((2, sz.d, sz.headp), bf16),
        VMEM((2, 2, 2, sz.half, sz.headp), f32), VMEM((2, 2, sz.half, sz.headp), bf16),
        VMEM((2, 2, sz.half, sz.headp), bf16), VMEM((2, sz.units, sz.part, sz.qkvp), bf16),
        VMEM((2, sz.d, sz.attnp), bf16), VMEM((2, sz.d, sz.ffw), bf16),
        VMEM((sz.d, sz.attnp), bf16), VMEM((sz.d, sz.ffw), bf16),
        VMEM((n, jumps) + attn_sum, bf16), VMEM((n, jumps) + ff_sum, bf16),
        VMEM((2, 2, sz.headp), f32), VMEM((2, 1, sz.ffp), f32), VMEM(own, f32), VMEM((2,) + ends, bf16),
        VMEM((n, deep, sz.d), f32), VMEM((sz.tp - 1, n, deep, sz.d), f32),
        VMEM((max(sz.ctx - 1, 1),) + small, f32), VMEM((jumps,) + small, f32), VMEM(small, f32), VMEM(small, f32),
        VMEM((2, deep, sz.d), f32), VMEM((deep, sz.d), f32),
        DMA((12 * n + 2,)), DMA((2 * n, sz.chunks, sz.fsdp, 2, sz.ctx)), DMA((2, 2, sz.images)), DMA((2, 2, sz.tp)),
        DMA((3, 2, far)), DMA((n, 2, 2)), DMA((2 * n, 2, sz.d // 128)), DMA((2,)),
    ] + team_scratch(sz, 2 * n)
    if sz.wrowsp != sz.wrows:
        padded = sz.groups * sz.wrowsp
        scratch += [VMEM((padded, sz.attnp), bf16), VMEM((padded, sz.ffw), bf16)]
    operands = (*saved, *wattn, *wff, cot, gains)
    return pl.pallas_call(
        functools.partial(backward_kernel, sz),
        out_shape=[jax.ShapeDtypeStruct(*s) for s in shapes],
        in_specs=[hbm] * (len(operands) - 2) + [vmem] * 2,
        out_specs=[hbm] * (2 * n + 1) + [vmem],
        scratch_shapes=scratch,
        compiler_params=params(2),
        name="backward",
    )(*operands)


def close_kernel(sz, *refs):
    n = sz.layers
    attn_refs, ff_refs, (whole_ref, small_ref), outs = split_refs(refs, n, n, 2, 11)
    out_ref, gin_ref, gain_ref, bias_ref, qkv_ref, qv_ref, wout_ref, up_ref, upb_ref, down_ref, resid_ref = outs
    full, ff = sz.wide * sz.zl, sz.ff * sz.zl

    def summed(ref):
        return [sum(ref[zh * sz.zl + j].astype(f32) for zh in range(sz.images)) for j in range(sz.zl)]

    def join(width, count, *runs):
        total = None
        for j, halves, start, lanes, place in [(j, *run) for run in runs for j in range(sz.zl)]:
            piece = shift_lanes(halves[j], start, lanes, j * count + place, up_to(width, 128))
            total = piece if total is None else total + piece
        return total[0:sz.wrows, 0:width]

    for layer in range(n):
        attn, hidden = summed(attn_refs[layer]), summed(ff_refs[layer])
        for kind in range(3):
            qkv_ref[layer, kind] = join(full, sz.wide, (attn, kind * sz.wide, sz.wide, 0))
        wout_ref[layer] = join(full, sz.wide, (attn, 3 * sz.wide, sz.wide, 0))
        rest = sz.ff - sz.spare
        first = [(attn, 4 * sz.wide, sz.spare, 0)] if sz.spare else []
        up_ref[layer] = join(ff, sz.ff, *first, (hidden, 0, rest, sz.spare))
        down_ref[layer] = join(ff, sz.ff, (hidden, rest, sz.ff, 0))
        values = small_ref[layer]
        gain_ref[layer] = values[0:2]
        bias_ref[layer] = values[2:4]
        resid_ref[layer] = values[4:6]
        total_qv, total_up = None, None
        for half in range(sz.zl):
            values = small_ref[n + half]
            qv = shift_lanes(values, 0, sz.wide, half * sz.wide, up_to(full, 128))
            up = shift_lanes(values, sz.ff_at, sz.ff, half * sz.ff, up_to(ff, 128))
            total_qv = qv if total_qv is None else total_qv + qv
            total_up = up if total_up is None else total_up + up
        qv_ref[layer] = total_qv[3 * layer:3 * layer + 2, 0:full]
        upb_ref[layer:layer + 1, :] = total_up[3 * layer + 2:3 * layer + 3, 0:ff]
    for image in range(sz.images):
        rows = whole_ref[0, :, image].reshape(sz.tp * sz.part, sz.d)
        out_ref[image] = rows[0:sz.rows]
        rows = whole_ref[1, :, image].reshape(sz.tp * sz.part, sz.d)
        gin_ref[image] = rows.astype(f32)[0:sz.rows]


def close_call(sz, attn_sums, ff_sums, ends, small):
    n, full, ff = sz.layers, sz.wide * sz.zl, sz.ff * sz.zl
    tokens = (sz.images, sz.rows, sz.d)
    vec, up = ((n, 2, sz.d), f32), ((n, sz.wrows, ff), f32)
    shapes = [
        (tokens, bf16), (tokens, f32), vec, vec, ((n, 3, sz.wrows, full), f32), ((n, 2, full), f32),
        ((n, sz.wrows, full), f32), up, ((n, ff), f32), up, vec,
    ]
    vmem = pl.BlockSpec(memory_space=pltpu.VMEM)
    results = pl.pallas_call(
        functools.partial(close_kernel, sz),
        out_shape=[jax.ShapeDtypeStruct(*s) for s in shapes],
        in_specs=[vmem] * (2 * n + 2),
        out_specs=[vmem] * len(shapes),
        compiler_params=pltpu.CompilerParams(vmem_limit_bytes=60 * 1024 * 1024),
        name="close",
    )(*attn_sums, *ff_sums, ends, small)
    results = list(results)
    results[4] = jnp.swapaxes(results[4], 1, 2)
    return tuple(results)


def per_device(mesh, inputs, cotangent, valid_count, norm_gain, norm_bias, w_qkv, bias_qv, w_out, w_up, bias_up,
               w_down, bias_resid):
    sz = Sizes(mesh, inputs, w_qkv, w_up)
    n = sz.layers
    *made, cot = forward_call(sz, valid_count, inputs, cotangent, jnp.swapaxes(w_qkv, 1, 2), w_out, w_up,
                              w_down, norm_gain, norm_bias, bias_qv, bias_up, bias_resid)
    saved, wattn, wff = split_refs(made, 11 * n, n, n)
    *sums, ends, small = backward_call(sz, saved, wattn, wff, cot, norm_gain)
    return close_call(sz, sums[:n], sums[n:], ends, small)


def solution(mesh):
    tokens, rows = P("fsdp", "ctx", None), P(None, ("fsdp", "ctx"), "tp")
    qkv = P(None, ("fsdp", "ctx"), None, "tp")
    qv, up = P(None, None, "tp"), P(None, "tp")
    return jax.shard_map(
        functools.partial(per_device, mesh),
        mesh=mesh,
        in_specs=(tokens, tokens, P("fsdp"), P(), P(), qkv, qv, rows, rows, up, rows, P()),
        out_specs=(tokens, tokens, P(), P(), qkv, qv, rows, rows, up, rows, P()),
        check_vma=False,
    )
```

profile of v0, /device:TPU:0, one launch (start us, length us, event | category | flops | bytes accessed | tf_op | source)
XLA Modules:
  0.0 372.9 jit_solution(685936456891206906)
XLA Ops:
  0.6 174.9 %forward.1 = (f32[2,48,1152]{2,1,0:T(8,128)}, f32[2,48,1152]{2,1,0:T(8,128)}, bf16[4,2,48,1152]{3,2,1,0:T(8,128)(2,1)}, bf16[4,2,48,1152]{3,2,1,0:T(8,128)(2,1)}...) custom-call(s32[2]{0:T(128)} %refs_0_.1, ...), custom_call_target="tpu_custom_call" | custom-call | tf_op jit(solution)/shard_map/forward/pallas_call | solution.py:1015
  175.5 190.6 %backward.1 = (bf16[4,144,640]{2,1,0:T(8,128)(2,1)}, bf16[4,144,640]{2,1,0:T(8,128)(2,1)}, bf16[4,144,1024]{2,1,0:T(8,128)(2,1)}, bf16[4,144,1024]{2,1,0:T(8,128...) custom-call(f32[2,48,1152]{2,1,0:T(8,128)} %get-tuple-element.55.refs_0_, ...), custom_call_target="tpu_custom_call" | custom-call | tf_op jit(solution)/shard_map/backward/pallas_call | solution.py:1469
  366.1 6.6 %close.1 = (bf16[2,184,1152]{2,1,0:T(8,128)(2,1)}, f32[2,184,1152]{2,1,0:T(8,128)}, f32[2,2,1152]{2,1,0:T(2,128)}, f32[2,2,1152]{2,1,0:T(2,128)}, f32[2,3,144,28...) custom-call(bf16[4,144,640]{2,1,0:T(8,128)(2,1)} %get-tuple-element., ...), custom_call_target="tpu_custom_call" | custom-call | tf_op jit(solution)/shard_map/close/pallas_call | solution.py:1534
where the time goes:
time: 373 us
  Pallas kernels  372 us (100%)
    pallas_call x1, Pallas kernels, backward_call(): pl.pallas_call(functools.partial(backward_kernel, sz), out_shape=[jax.Sha...  191 us
    pallas_call x1, Pallas kernels, forward_call(): pl.pallas_call(functools.partial(forward_kernel, sz), out_shape=[jax.Shap...  175 us

commit v1 on v0

--- a/solution.py
+++ b/solution.py
@@ -715,15 +715,11 @@
 
     def project(step, carry):
         units, tokens = gather.ready(step)
-
-        def shard(s, none):
+        for s in range(2):
             both3 = dot(tokens, w_ref[s, :, 0:sz.qkvp], (1, 0))
             put_rows(sz, q_ref.at[s], units, (take(sz, both3, 0) + qv_ref[s, 0:1, 0:sz.headp]).astype(bf16))
             put_rows(sz, k_ref.at[s, pc.k], units, take(sz, both3, 1).astype(bf16))
             put_rows(sz, v_ref.at[s, pc.k], units, (take(sz, both3, 2) + qv_ref[s, 1:2, 0:sz.headp]).astype(bf16))
-            return none
-
-        lax.fori_loop(0, 2, shard, 0)
         jobs.at("project", step)
         return carry
 
@@ -744,8 +740,8 @@
 
     def attend(step, carry):
         units = scatter.units(step)
-
-        def shard(s, partial):
+        partial = None
+        for s in range(2):
             keys = k_ref[s].reshape(sz.keys, sz.headp)
             values = v_ref[s].reshape(sz.keys, sz.headp)
             queries = rows_of(q_ref.at[s], units)
@@ -755,9 +751,8 @@
                 total = total + dot(probs.astype(bf16), head_of(values, head), (1, 0))
             mixed = total.astype(bf16)
             put_rows(sz, mixed_ref.at[s], units, mixed)
-            return partial + dot(mixed, o_ref[s], (1, 1))
-
-        partial = lax.fori_loop(0, 2, shard, jnp.zeros((sz.tile, sz.d), f32))
+            terms = dot(mixed, o_ref[s], (1, 1))
+            partial = terms if partial is None else partial + terms
         scatter.push(step, partial)
         jobs.at("attend", step)
         return carry
@@ -773,8 +768,8 @@
 
     def feed(step, carry):
         units, tokens = gather.ready(step)
-
-        def shard(s, partial):
+        partial = None
+        for s in range(2):
             pre = dot(tokens, w_ref[s, :, 0:sz.ffp], (1, 0)) + upb_ref[s, 2:3, 0:sz.ffp]
             put_rows(sz, pre_ref.at[s], units, pre)
             hidden = 0.5 * pre * (1.0 + jnp.tanh(gelu_root * (pre + gelu_cubic * pre * pre * pre)))
@@ -783,9 +778,8 @@
                 hidden = pltpu.roll(hidden, (sz.down_shift - sz.ff_at) % sz.ffp, 1)
             hidden = hidden.astype(bf16)
             put_rows(sz, hidden_ref.at[s], units, hidden)
-            return partial + dot(hidden, w_ref[s, :, sz.down_at:], (1, 1))
-
-        partial = lax.fori_loop(0, 2, shard, jnp.zeros((sz.tile, sz.d), f32))
+            terms = dot(hidden, w_ref[s, :, sz.down_at:], (1, 1))
+            partial = terms if partial is None else partial + terms
         scatter.push(step, partial)
         jobs.at("feed", step)
         return carry
@@ -811,7 +805,7 @@
     return steps
 
 
-GIVE_FF = (("s0", "", "t0"), ("s1", "", "d2 t1"), ("s3", "", "t2"))
+GIVE_FF = (("s1", "", "d2 t0"), ("s2", "", "t1"), ("s3", "", "t2"))
 GIVE_ATTN = (("s0", "t0", ""), ("s1", "d2", ""), ("s2", "t1", ""), ("s3", "t2", ""))
 PLAN_ATTN_FIRST = (("s0", "d2", ""), ("s3", "t1", ""), ("m0", "l0", ""), ("m1", "", "d0"), ("m2", "t2 l1", ""),
                    ("m3", "", "d1"), ("f", "l2", "d2 t0"))

time: 373 us -> 369 us (0.989)
  Pallas kernels: 372 us -> 368 us
where the time goes in v1:
time: 369 us
  Pallas kernels  368 us (100%)
    pallas_call x1, Pallas kernels, backward_call(): pl.pallas_call(functools.partial(backward_kernel, sz), out_shape=[jax.Sha...  190 us
    pallas_call x1, Pallas kernels, forward_call(): pl.pallas_call(functools.partial(forward_kernel, sz), out_shape=[jax.Shap...  171 us

profile of v1, /device:TPU:0, one launch (start us, length us, event | category | flops | bytes accessed | tf_op | source)
XLA Modules:
  0.0 368.7 jit_solution(9996910694017297566)
XLA Ops:
  0.6 171.3 %forward.1 = (f32[2,48,1152]{2,1,0:T(8,128)}, f32[2,48,1152]{2,1,0:T(8,128)}, bf16[4,2,48,1152]{3,2,1,0:T(8,128)(2,1)}, bf16[4,2,48,1152]{3,2,1,0:T(8,128)(2,1)}...) custom-call(s32[2]{0:T(128)} %refs_0_.1, ...), custom_call_target="tpu_custom_call" | custom-call | tf_op jit(solution)/shard_map/forward/pallas_call | solution.py:1009
  172.0 189.9 %backward.1 = (bf16[4,144,640]{2,1,0:T(8,128)(2,1)}, bf16[4,144,640]{2,1,0:T(8,128)(2,1)}, bf16[4,144,1024]{2,1,0:T(8,128)(2,1)}, bf16[4,144,1024]{2,1,0:T(8,128...) custom-call(f32[2,48,1152]{2,1,0:T(8,128)} %get-tuple-element.55.refs_0_, ...), custom_call_target="tpu_custom_call" | custom-call | tf_op jit(solution)/shard_map/backward/pallas_call | solution.py:1463
  361.9 6.6 %close.1 = (bf16[2,184,1152]{2,1,0:T(8,128)(2,1)}, f32[2,184,1152]{2,1,0:T(8,128)}, f32[2,2,1152]{2,1,0:T(2,128)}, f32[2,2,1152]{2,1,0:T(2,128)}, f32[2,3,144,28...) custom-call(bf16[4,144,640]{2,1,0:T(8,128)(2,1)} %get-tuple-element., ...), custom_call_target="tpu_custom_call" | custom-call | tf_op jit(solution)/shard_map/close/pallas_call | solution.py:1528

commit v2 on v1

--- a/solution.py
+++ b/solution.py
@@ -173,7 +173,7 @@
 
 FORWARD_TURN = (False, True)
 BACKWARD_TURN = (True, False)
-SUM_TURN = (True, True)
+SUM_TURN = (True, False)
 
 
 class Routes:
@@ -807,7 +807,7 @@
 
 GIVE_FF = (("s1", "", "d2 t0"), ("s2", "", "t1"), ("s3", "", "t2"))
 GIVE_ATTN = (("s0", "t0", ""), ("s1", "d2", ""), ("s2", "t1", ""), ("s3", "t2", ""))
-PLAN_ATTN_FIRST = (("s0", "d2", ""), ("s3", "t1", ""), ("m0", "l0", ""), ("m1", "", "d0"), ("m2", "t2 l1", ""),
+PLAN_ATTN_FIRST = (("s2", "t1", ""), ("m0", "l0", ""), ("m1", "", "d0"), ("m2", "t2 l1", ""),
                    ("m3", "", "d1"), ("f", "l2", "d2 t0"))
 PLAN_ATTN = (("s1", "t1", "d0"), ("s2", "d2", ""), ("s3", "l0", ""), ("m0", "", "d1"), ("m1", "t2 l1", ""),
              ("m3", "", "d2"), ("f", "l2", "t0"))
@@ -909,7 +909,7 @@
     for layer in range(1, n):
         pack_ff(layer)
     attn[0].run("l1")
-    ff[0].run("t0")
+    ff[0].run("t0 d2")
     attn[0].run("l2")
     for move in bias_swaps:
         move.wait()
@@ -1473,8 +1473,13 @@
 
 def close_kernel(sz, *refs):
     n = sz.layers
-    attn_refs, ff_refs, (whole_ref, small_ref), outs = split_refs(refs, n, n, 2, 11)
-    out_ref, gin_ref, gain_ref, bias_ref, qkv_ref, qv_ref, wout_ref, up_ref, upb_ref, down_ref, resid_ref = outs
+    attn_ins, ff_ins, (whole_in, small_ref), outs, scratch = split_refs(refs, n, n, 2, 11, 10)
+    out_to, gin_to, gain_ref, bias_ref, qkv_to, qv_ref, wout_to, up_to_, upb_ref, down_to, resid_ref = outs
+    attn_refs, ff_refs, whole_ref, out_ref, gin_ref, qkv_ref, wout_ref, up_ref, down_ref, sems = scratch
+    copies = Copies(sems)
+    whole_load = copies.start(whole_in, whole_ref)
+    loads = [[copies.start(attn_ins[l], attn_refs.at[l]), copies.start(ff_ins[l], ff_refs.at[l])] for l in range(n)]
+    arrived = [whole_load] + sum(loads, [])
     full, ff = sz.wide * sz.zl, sz.ff * sz.zl
 
     def summed(ref):
@@ -1487,8 +1492,17 @@
             total = piece if total is None else total + piece
         return total[0:sz.wrows, 0:width]
 
+    copies.wait([whole_load])
+    for image in range(sz.images):
+        rows = whole_ref[0, :, image].reshape(sz.tp * sz.part, sz.d)
+        out_ref[image] = rows[0:sz.rows]
+        rows = whole_ref[1, :, image].reshape(sz.tp * sz.part, sz.d)
+        gin_ref[image] = rows.astype(f32)[0:sz.rows]
+    copies.start(out_ref, out_to)
+    copies.start(gin_ref, gin_to)
     for layer in range(n):
-        attn, hidden = summed(attn_refs[layer]), summed(ff_refs[layer])
+        copies.wait(loads[layer])
+        attn, hidden = summed(attn_refs.at[layer]), summed(ff_refs.at[layer])
         for kind in range(3):
             qkv_ref[layer, kind] = join(full, sz.wide, (attn, kind * sz.wide, sz.wide, 0))
         wout_ref[layer] = join(full, sz.wide, (attn, 3 * sz.wide, sz.wide, 0))
@@ -1496,6 +1510,8 @@
         first = [(attn, 4 * sz.wide, sz.spare, 0)] if sz.spare else []
         up_ref[layer] = join(ff, sz.ff, *first, (hidden, 0, rest, sz.spare))
         down_ref[layer] = join(ff, sz.ff, (hidden, rest, sz.ff, 0))
+        for ref, to in ((qkv_ref, qkv_to), (wout_ref, wout_to), (up_ref, up_to_), (down_ref, down_to)):
+            copies.start(ref.at[layer], to.at[layer])
         values = small_ref[layer]
         gain_ref[layer] = values[0:2]
         bias_ref[layer] = values[2:4]
@@ -1509,11 +1525,7 @@
             total_up = up if total_up is None else total_up + up
         qv_ref[layer] = total_qv[3 * layer:3 * layer + 2, 0:full]
         upb_ref[layer:layer + 1, :] = total_up[3 * layer + 2:3 * layer + 3, 0:ff]
-    for image in range(sz.images):
-        rows = whole_ref[0, :, image].reshape(sz.tp * sz.part, sz.d)
-        out_ref[image] = rows[0:sz.rows]
-        rows = whole_ref[1, :, image].reshape(sz.tp * sz.part, sz.d)
-        gin_ref[image] = rows.astype(f32)[0:sz.rows]
+    copies.wait([i for i in range(len(copies.made)) if i not in arrived])
 
 
 def close_call(sz, attn_sums, ff_sums, ends, small):
@@ -1524,12 +1536,16 @@
         (tokens, bf16), (tokens, f32), vec, vec, ((n, 3, sz.wrows, full), f32), ((n, 2, full), f32),
         ((n, sz.wrows, full), f32), up, ((n, ff), f32), up, vec,
     ]
-    vmem = pl.BlockSpec(memory_space=pltpu.VMEM)
+    vmem, hbm = pl.BlockSpec(memory_space=pltpu.VMEM), pl.BlockSpec(memory_space=pl.ANY)
     results = pl.pallas_call(
         functools.partial(close_kernel, sz),
         out_shape=[jax.ShapeDtypeStruct(*s) for s in shapes],
-        in_specs=[vmem] * (2 * n + 2),
-        out_specs=[vmem] * len(shapes),
+        in_specs=[hbm] * (2 * n + 1) + [vmem],
+        out_specs=[hbm, hbm, vmem, vmem, hbm, vmem, hbm, hbm, vmem, hbm, vmem],
+        scratch_shapes=[
+            VMEM((n,) + attn_sums[0].shape, bf16), VMEM((n,) + ff_sums[0].shape, bf16), VMEM(ends.shape, bf16),
+            *[VMEM(*shapes[i]) for i in (0, 1, 4, 6, 7, 9)], DMA((6 * n + 3,)),
+        ],
         compiler_params=pltpu.CompilerParams(vmem_limit_bytes=60 * 1024 * 1024),
         name="close",
     )(*attn_sums, *ff_sums, ends, small)

time: 369 us -> 366 us (level)
  Pallas kernels: 368 us -> 364 us
    pallas_call x1, Pallas kernels: 190 us -> 183 us  [backward_call(): pl.pallas_call(functools.partial(backward_kernel, sz), out_shape=[jax.Sha...]
where the time goes in v2:
time: 366 us; the launch traced here: 365 us
  Pallas kernels  364 us (99%)
    pallas_call x1, Pallas kernels, backward_call(): pl.pallas_call(functools.partial(backward_kernel, sz), out_shape=[jax.Sha...  183 us
    pallas_call x1, Pallas kernels, forward_call(): pl.pallas_call(functools.partial(forward_kernel, sz), out_shape=[jax.Shap...  174 us

profile of v2, /device:TPU:0, one launch (start us, length us, event | category | flops | bytes accessed | tf_op | source)
XLA Modules:
  0.0 364.6 jit_solution(14300654634933018105)
XLA Ops:
  0.6 174.4 %forward.1 = (f32[2,48,1152]{2,1,0:T(8,128)}, f32[2,48,1152]{2,1,0:T(8,128)}, bf16[4,2,48,1152]{3,2,1,0:T(8,128)(2,1)}, bf16[4,2,48,1152]{3,2,1,0:T(8,128)(2,1)}...) custom-call(s32[2]{0:T(128)} %refs_0_.1, ...), custom_call_target="tpu_custom_call" | custom-call | tf_op jit(solution)/shard_map/forward/pallas_call | solution.py:1009
  175.0 182.9 %backward.1 = (bf16[4,144,640]{2,1,0:T(8,128)(2,1)}, bf16[4,144,640]{2,1,0:T(8,128)(2,1)}, bf16[4,144,1024]{2,1,0:T(8,128)(2,1)}, bf16[4,144,1024]{2,1,0:T(8,128...) custom-call(f32[2,48,1152]{2,1,0:T(8,128)} %get-tuple-element.55.refs_0_, ...), custom_call_target="tpu_custom_call" | custom-call | tf_op jit(solution)/shard_map/backward/pallas_call | solution.py:1463
  357.9 6.5 %close.1 = (bf16[2,184,1152]{2,1,0:T(8,128)(2,1)}, f32[2,184,1152]{2,1,0:T(8,128)}, f32[2,2,1152]{2,1,0:T(2,128)}, f32[2,2,1152]{2,1,0:T(2,128)}, f32[2,3,144,28...) custom-call(bf16[4,144,640]{2,1,0:T(8,128)(2,1)} %get-tuple-element., ...), custom_call_target="tpu_custom_call" | custom-call | tf_op jit(solution)/shard_map/close/pallas_call | solution.py:1540
